TPU v7x, 256 devices: a whole 4x4x8 slice. The times are simulated.
256 devices in a mesh: mem: 64 (over y, z, core), sub: 4 (over x).
Axes of the slice: x: 4, y: 4, z: 8, core: 2. Of those that a mesh axis runs over, the one named last changes fastest.
Arguments:
- prior_realizations: float32 [128, 1024, 1024], P('mem', 'sub'), may hold values from -0.6 to 0.6
- soaked_part_table: float32 [128], P('mem'), may hold values from 0.15 to 0.6
- sightline_crossed_boxes: int32 [4, 64, 32], P('sub'), may hold values from 0 to 262143
- sightline_step_amount: int32 [4, 64], P('sub'), may hold values from 1 to 32, as said below
- camera_tile_displacement: int32 [4, 64, 128], P('sub'), may hold values from 0 to 4095
- camera_kelvin_data: float32 [4, 64, 128], P('sub', 'mem'), may hold values from -2 to 2
- camera_reciprocal_spread: float32 [4, 64, 128], P('sub', 'mem'), may hold values from 0.25 to 2
Outputs:
- analysis: float32 [128, 1024, 1024], P('mem', 'sub')
Inputs may be any that keep to these rules, and one draw needn't show every extreme that they name: `sightline_step_amount`: every subdomain has a ray of 32 cells. `sightline_crossed_boxes`: row-major cell of the subdomain's 256 x 1024 block. `camera_tile_displacement`: cell within brick j of subdomain s.
All inputs are finite; a program needn't handle non-finite values.
Results may differ from a plain program's by a relative error of at most 0.0003.
Values sent between devices are 32-bit elements; how exact they have to be, the bound alone decides.
A program may use at most 320 MiB of HBM per device.

v0:
```python
import math

import jax
import jax.numpy as jnp
from jax import lax
from jax.sharding import PartitionSpec as P

ITERS = 20


conduct = 0.2


def padded_2(shard, sides, width):
    for axis, dim in sides:
        devices, length = (lax.axis_size(axis), shard.shape[dim])
        up = [(i, (i + 1) % devices) for i in range(devices - 1)]
        down = [(j, i) for i, j in up]
        last = lax.slice_in_dim(shard, length - width, length, axis=dim)
        leading = lax.slice_in_dim(shard, 0, width, axis=dim)
        before = lax.ppermute(last, axis, up)
        after = lax.ppermute(leading, axis, down)
        shard = jnp.concatenate([before, shard, after], axis=dim)
    return shard


def along_z(kelvin_mesh):
    padded = jnp.pad(kelvin_mesh, ((0, 0), (0, 0), (1, 1)))
    return padded[:, :, 2:] + padded[:, :, :-2] - 2.0 * kelvin_mesh


def ensemble_weights(gram_sum, pull_sum):
    members = gram_sum.shape[0]
    identity = jnp.eye(members, dtype=jnp.float32)
    system = (members - 1.0) * identity + gram_sum
    norm_scale = jnp.sqrt(jnp.sum(system * system))

    def newton_body(index_step, carry_pair):
        upper_iter, lower_iter = carry_pair
        newton_step = 1.5 * identity - 0.5 * jnp.dot(
            lower_iter, upper_iter, precision=lax.Precision.HIGHEST
        )
        return (
            jnp.dot(upper_iter, newton_step, precision=lax.Precision.HIGHEST),
            jnp.dot(newton_step, lower_iter, precision=lax.Precision.HIGHEST),
        )

    upper_iter, lower_iter = lax.fori_loop(0, ITERS, newton_body, (system / norm_scale, identity))
    inv_root = lower_iter / jnp.sqrt(norm_scale)
    mean_shift = jnp.dot(
        inv_root,
        jnp.dot(inv_root, pull_sum, precision=lax.Precision.HIGHEST),
        precision=lax.Precision.HIGHEST,
    )
    return math.sqrt(members - 1.0) * inv_root + mean_shift[:, None]


def caloric_spread_step(kelvin_mesh, melting_power_feed):
    padded = padded_2(kelvin_mesh, (("sub", 1),), 1)
    across = padded[:, 2:] + padded[:, :-2] - 2.0 * kelvin_mesh
    return kelvin_mesh + conduct * (across + along_z(kelvin_mesh)) + melting_power_feed


def body(
    prior_realizations,
    soaked_part_table,
    sightline_crossed_boxes,
    sightline_step_amount,
    camera_tile_displacement,
    camera_kelvin_data,
    camera_reciprocal_spread,
):
    realization_parts, tile_stripes, upward_reach = prior_realizations.shape
    seg_total = sightline_crossed_boxes.shape[2]
    seg_index = jnp.arange(seg_total, dtype=jnp.int32)
    live_mask = (seg_index[None, :] < sightline_step_amount[0][:, None]).astype(jnp.float32)
    fade_rate = (
        soaked_part_table[:, None]
        * (1.0 - soaked_part_table[:, None]) ** seg_index.astype(jnp.float32)[None, :]
    )
    amount = (fade_rate[:, None, :] * live_mask[None]).reshape(realization_parts, -1)
    melting_power_feed = (
        jnp.zeros((realization_parts, tile_stripes * upward_reach), jnp.float32)
        .at[:, sightline_crossed_boxes[0].reshape(-1)]
        .add(amount)
    )
    melting_power_feed = melting_power_feed.reshape(realization_parts, tile_stripes, upward_reach)
    kelvin_mesh = caloric_spread_step(prior_realizations, melting_power_feed)
    kelvin_mesh = caloric_spread_step(kelvin_mesh, melting_power_feed)
    flat_field = kelvin_mesh.reshape(realization_parts, tile_stripes * upward_reach)
    gathered = lax.all_to_all(flat_field, "mem", split_axis=1, concat_axis=0, tiled=True)
    members = gathered.shape[0]
    mean_field = jnp.sum(gathered, axis=0) / members
    pert_field = gathered - mean_field[None]
    eigen_spectrum = camera_kelvin_data[0, 0]
    own_weight = camera_reciprocal_spread[0, 0]
    obs_rows = lax.dynamic_index_in_dim(
        camera_tile_displacement[0], lax.axis_index("mem"), 0, keepdims=False
    )
    seen_pert = pert_field[:, obs_rows]
    predicted_average = mean_field[obs_rows]
    discrepancy = eigen_spectrum - predicted_average
    weighted = seen_pert * own_weight[None]
    gram_part = jnp.dot(weighted, seen_pert.T, precision=lax.Precision.HIGHEST)
    pull_part = jnp.dot(weighted, discrepancy, precision=lax.Precision.HIGHEST)
    gram_sum, pull_sum = lax.psum((gram_part, pull_part), ("mem", "sub"))
    transform = ensemble_weights(gram_sum, pull_sum)
    analysed = mean_field[None] + jnp.dot(transform.T, pert_field, precision=lax.Precision.HIGHEST)
    returned = lax.all_to_all(analysed, "mem", split_axis=0, concat_axis=1, tiled=True)
    return returned.reshape(realization_parts, tile_stripes, upward_reach)


def solution(mesh):
    placed = (
        P("mem", "sub", None),
        P("mem"),
        P("sub", None, None),
        P("sub", None),
        P("sub", None, None),
        P("sub", "mem", None),
        P("sub", "mem", None),
    )
    return jax.shard_map(
        body, mesh=mesh, in_specs=placed, out_specs=P("mem", "sub", None), check_vma=False
    )
```

profile of v0, /device:TPU:1, one launch (start us, length us, event | category | flops | bytes accessed | tf_op | source)
XLA Modules:
  0.0 600.0 jit_solution(16836463082684447646)
XLA Ops:
  6.5 0.9 fusion.40
  7.4 1.3 collective-permute-start
  8.7 4.6 collective-permute-start.1
  13.3 0.8 copy.21
  14.2 4.4 sort
  21.4 79.6 %scatter_custom_fusion = f32[2,262144]{0,1:T(8,128)} fusion(s32[2048]{0:T(1024)S(1)} %get-tuple-element.45, f32[]{:T(128)} %constant.9.clone.1, f32[2048,2]{1,0:T(8,128)S(1)} %bitcast.62, s32[2048]{0:T(1024)S(1)} %broadcast_clamp_fusion), kind=kCustom, calls=%fused_computation.9 | custom fusion | flops 4096 | bytes 2097156 | tf_op jit(solution)/shard_map/scatter-add | solution.py:85
  101.0 72.7 %copy.23 = f32[2,256,1024]{2,1,0:T(8,128)S(1)} copy(f32[2,256,1024]{0,2,1:T(8,128)} %bitcast.4) | data formatting | bytes 4194304 | tf_op jit(solution)/shard_map/reshape | solution.py:87
  173.7 6.0 %fusion.11 = f32[2,256,1024]{2,1,0:T(8,128)S(1)} fusion(f32[2,256,1024]{2,1,0:T(8,128)S(1)} %copy.23, f32[2,256,1024]{2,1,0:T(8,128)} %param.9, f32[2,1,1024]{2,1,0:T(1,128)S(1)} %collective-permute-done.1, f32[2,1,1024]{2,1,0:T(1,128)S(1)} %collective-permute-done), kind=kLoop, calls=%fused_computation.21 | loop fusion | flops 5767168 | bytes 6307840 | tf_op jit(solution)/shard_map/add | solution.py:61
  179.8 1.3 collective-permute-start.2
  181.1 4.0 collective-permute-start.3
  185.8 2.5 fusion.17
  188.3 2.2 all_to_all.26
  190.5 2.9 copy.25
  193.5 14.3 %all-to-all-start = ((f32[2,64,4096]{2,0,1:T(2,128)}), f32[2,64,4096]{2,0,1:T(2,128)S(1)}, u32[]{:S(2)}, u32[]{:S(2)}) async-start(f32[2,64,4096]{2,0,1:T(2,128)} %copy.25), calls=%async_computation | async-start | bytes 4194304 | tf_op jit(solution)/shard_map/all_to_all | solution.py:91
  208.5 50.5 %all-to-all-done = f32[2,64,4096]{2,0,1:T(2,128)S(1)} async-done(((f32[2,64,4096]{2,0,1:T(2,128)}), f32[2,64,4096]{2,0,1:T(2,128)S(1)}, u32[]{:S(2)}, u32[]{:S(2)}) %all-to-all-start) | async-done | bytes 2097184 | tf_op jit(solution)/shard_map/all_to_all | solution.py:91
  259.0 0.9 reduce_sum.18
  260.3 2.7 all_to_all.29
  263.0 1.5 broadcast_subtract_fusion
  264.5 3.0 copy.26
  267.5 1.1 gather_fusion.1
  268.6 2.2 gather_fusion
  270.9 1.0 fusion.25
  272.1 77.3 %psum.15 = f32[128]{0:T(128)S(1)} all-reduce(f32[128]{0:T(128)S(1)} %convolution_bitcast_fusion.3), channel_id=1, replica_groups=mesh['mem'=64,'sub'=4] {'mem','sub'}, use_global_device_ids=true, to_apply=%region_6.7 | all-reduce | flops 128 | bytes 1024 | tf_op jit(solution)/shard_map/psum | solution.py:106
  349.4 158.1 %all-reduce.4.cloned.1.call-done = f32[128,128]{1,0:T(8,128)} async-done(((f32[128,128]{1,0:T(8,128)}), f32[128,128]{1,0:T(8,128)}) %all-reduce.4.cloned.1.call-update) | async-done | bytes 65552 | tf_op jit(solution)/shard_map/psum | solution.py:106
  507.5 1.5 multiply_reduce_fusion
  509.7 0.9 fusion.30
  510.7 16.3 %while.13 = (s32[]{:T(128)}, f32[128,128]{0,1:T(8,128)S(1)}, f32[128,128]{1,0:T(8,128)S(1)}, s32[]{:T(128)}) while((s32[]{:T(128)}, f32[128,128]{0,1:T(8,128)S(1)}, f32[128,128]{1,0:T(8,128)S(1)}, s32[]{:T(128)}) %tuple.26), condition=%wide.region_5.6_spmd.clone, body=%wide.region_4.5_spmd.clone.sunk | while | flops 75563008 | bytes 852021 | solution.py:48
  527.5 3.4 convolution_add_fusion
  530.8 2.5 all_to_all.30
  533.3 57.0 %all_to_all.35 = f32[64,2,4096]{2,1,0:T(2,128)S(1)} all-to-all(f32[64,2,4096]{2,1,0:T(2,128)S(1)} %all_to_all.30), channel_id=1, replica_groups=mesh['mem'=64,'sub'=4] {'mem'}, dimensions={0} | all-to-all | bytes 4194304 | tf_op jit(solution)/shard_map/all_to_all | solution.py:109
  590.3 1.2 copy.28
  591.5 1.6 reshape.144
  (135 shorter events, 21.0 us)
Async XLA Ops:
  7.4 166.3 %collective-permute-start = (f32[2,1,1024]{2,1,0:T(1,128)S(1)}, f32[2,1,1024]{2,1,0:T(1,128)S(1)}, u32[]{:S(2)}, u32[]{:S(2)}) collective-permute-start(f32[2,1,1024]{2,1,0:T(1,128)S(1)} %get-tuple-element.55), channel_id=1, source_target_pairs={{1,0},{2,1},{3,2},{5,4},{6,5},{7,6},{9,8},{10,9},{11,10},{13,12},{... | collective-permute-start | bytes 24584 | tf_op jit(solution)/shard_map/ppermute | solution.py:22
  8.7 165.0 %collective-permute-start.1 = (f32[2,1,1024]{2,1,0:T(1,128)S(1)}, f32[2,1,1024]{2,1,0:T(1,128)S(1)}, u32[]{:S(2)}, u32[]{:S(2)}) collective-permute-start(f32[2,1,1024]{2,1,0:T(1,128)S(1)} %get-tuple-element.56), channel_id=1, source_target_pairs={{0,1},{1,2},{2,3},{4,5},{5,6},{6,7},{8,9},{9,10},{10,11},{12,13},{... | collective-permute-start | bytes 24584 | tf_op jit(solution)/shard_map/ppermute | solution.py:21
  179.8 5.3 collective-permute-start.2
  181.1 4.8 collective-permute-start.3
  193.5 65.5 %all-to-all-start = ((f32[2,64,4096]{2,0,1:T(2,128)}), f32[2,64,4096]{2,0,1:T(2,128)S(1)}, u32[]{:S(2)}, u32[]{:S(2)}) async-start(f32[2,64,4096]{2,0,1:T(2,128)} %copy.25), calls=%async_computation | async-start | bytes 4194304 | tf_op jit(solution)/shard_map/all_to_all | solution.py:91
  207.7 299.8 %all-reduce.4.cloned.1.call-start = ((), (), s32[]{:S(2)}) async-start(), calls=%async_computation.2 | async-start | bytes 131072 | tf_op jit(solution)/shard_map/psum | solution.py:106
  259.0 1.3 copy-start
  264.5 6.4 %copy-start.1 = (f32[1,1,128]{2,1,0:T(1,128)S(1)}, f32[1,1,128]{2,1,0:T(1,128)}, u32[]{:S(2)}) copy-start(f32[1,1,128]{2,1,0:T(1,128)} %param.15) | copy-start | bytes 1540
  264.5 7.4 %copy-start.2 = (f32[1,1,128]{2,1,0:T(1,128)S(1)}, f32[1,1,128]{2,1,0:T(1,128)}, u32[]{:S(2)}) copy-start(f32[1,1,128]{2,1,0:T(1,128)} %param.14) | copy-start | bytes 1540
Sparse Core Ops, SparseCore 0:
  272.0 235.4 all-reduce.3
where the time goes:
time: 602 us; the launch traced here: 600 us
  waiting for transfers between devices  209 us (35%)
  blocking collectives  134 us (22%)
  other arithmetic  99.7 us (17%)
  local copies, waits for them, and re-layouts  95.8 us (16%)
  starting transfers between devices  25.4 us (4%)
  matrix products  20.1 us (3%)
  between operations  14.4 us (2%)
    psum x1, waiting for transfers between devices, body(): gram_sum, pull_sum = lax.psum((gram_part, pull_part), ('mem', 'sub'))  158 us
    scatter-add x3, other arithmetic, body(): melting_power_feed = jnp.zeros((realization_parts, tile_stripes * upward_...  84 us
    psum x1, blocking collectives, body(): gram_sum, pull_sum = lax.psum((gram_part, pull_part), ('mem', 'sub'))  77.3 us
    reshape x1, local copies, waits for them, and re-layouts, body(): melting_power_feed.reshape(realization_parts, tile_stripes, upward_reach)  72.7 us
    all_to_all x1, blocking collectives, body(): lax.all_to_all(analysed, 'mem', split_axis=0, concat_axis=1, tiled=True)  57 us
    all_to_all x1, waiting for transfers between devices, body(): lax.all_to_all(flat_field, 'mem', split_axis=1, concat_axis=0, tiled=True)  50.5 us
    all_to_all x1, starting transfers between devices, body(): lax.all_to_all(flat_field, 'mem', split_axis=1, concat_axis=0, tiled=True)  14.3 us
  transfers between devices with their start and end apart: 6, of which 3 were waited for; matrix products, arithmetic and copies ran while one was open for 27% of the time, Pallas kernels for 0%

commit v1 on v0

v1 whole, which is shorter than its diff:
```python
import functools
import math

import jax
import jax.numpy as jnp
from jax import lax
from jax.experimental import pallas as pl
from jax.experimental.pallas import tpu as pltpu
from jax.sharding import PartitionSpec as P

MESH = pl.DeviceIdType.MESH
HIGHEST = lax.Precision.HIGHEST
ITERS = 20
CONDUCT = 0.2
F32, BF16, I32 = jnp.float32, jnp.bfloat16, jnp.int32
N_MEM, N_SUB = 64, 4
ROWS, COLS = 256, 1024
SEG, RAYS = 32, 64
PIX = 128
BLOCK = 32
STEP = 27
BATCHES = (12, 19, 26, 33, 40, 64)


def dot(a, b, precision=None):
    return jnp.dot(a, b, preferred_element_type=F32, precision=precision)


def iota(shape, dim):
    return lax.broadcasted_iota(I32, shape, dim)


def split(x):
    hi = x.astype(BF16)
    return hi, (x - hi.astype(F32)).astype(BF16)


def fades(share, shape):
    k = iota(shape, 1)
    base = jnp.broadcast_to(1.0 - share, shape)
    out = jnp.broadcast_to(share, shape)
    for bit in range(5):
        out = jnp.where(((k >> bit) & 1) == 1, out * base, out)
        base = base * base
    return out


def spread(v):
    col = iota(v.shape, 1)
    n = v.shape[0]
    left = jnp.where(col == 0, 0.0, pltpu.roll(v, 1, 1))
    right = jnp.where(col == COLS - 1, 0.0, pltpu.roll(v, COLS - 1, 1))
    return CONDUCT * (v + pltpu.roll(v, 1, 0) + pltpu.roll(v, n - 1, 0) + left + right)


def kernel(
    prior, share, cells, steps, pixel, kelvin, weight,
    out, extra,
    field, halo_s, halo_t, flown, onehot, amount_hi, amount_lo,
    pix, pix_in, gram_out, gram_in, part_in, full,
    got, got_hi, got_lo, grid_hi, grid_lo, back,
    load_sem, up_sem, down_sem, big_send, big_recv, pix_send, pix_recv,
    gram_send, gram_recv, part_send, part_recv, full_send, full_recv, back_send, back_recv,
):
    me, sub = lax.axis_index("mem"), lax.axis_index("sub")
    y, zc = me // 16, lax.rem(me, 16)
    q = y * N_SUB + sub

    def plane_peer(i):
        return lax.rem(me + i, N_MEM)

    def xy_peer(p):
        return ((p // N_SUB) * 16 + zc, lax.rem(p, N_SUB))

    def zc_peer(p):
        return (y * 16 + p, sub)

    above = (me, lax.rem(sub + N_SUB - 1, N_SUB))
    below = (me, lax.rem(sub + 1, N_SUB))

    barrier = pltpu.get_barrier_semaphore()

    @pl.loop(1, N_MEM)
    def _(i):
        pl.semaphore_signal(barrier, inc=1, device_id=(plane_peer(i), sub), device_id_type=MESH)

    @pl.loop(1, 16)
    def _(i):
        pl.semaphore_signal(barrier, inc=1, device_id=xy_peer(lax.rem(q + i, 16)), device_id_type=MESH)

    load = pltpu.make_async_copy(prior, field.at[:, pl.ds(8, ROWS)], load_sem)
    load.start()

    lanes = iota((RAYS, COLS), 1)
    upright = jnp.transpose(cells[...])
    for k in range(SEG):
        col = upright[:, k : k + 1] & (COLS - 1)
        onehot[k * RAYS : (k + 1) * RAYS, :] = jnp.where(lanes == col, 1.0, 0.0).astype(BF16)

    quad = [
        jnp.concatenate([cells[4 * c + i : 4 * c + i + 1, :] for i in range(4)], axis=1)
        for c in range(8)
    ]
    live_steps = jnp.concatenate([steps[...]] * 4, axis=1)

    def amounts(fade8):
        for c in range(8):
            step = iota((SEG, 256), 1) // RAYS + 4 * c
            grown = jnp.where(iota((SEG, 256), 0) == step, 1.0, 0.0)
            value = dot(fade8, grown, HIGHEST)
            value = jnp.where(step[:1] < live_steps, value, 0.0)
            hit = iota((ROWS, 256), 0) == (quad[c] >> 10)
            for m in range(2):
                row = value[m : m + 1, :]
                hi = row.astype(BF16).astype(F32)
                here = (slice(m * ROWS, (m + 1) * ROWS), slice(c * 256, (c + 1) * 256))
                amount_hi[here] = jnp.where(hit, hi, 0.0).astype(BF16)
                amount_lo[here] = jnp.where(hit, row - hi, 0.0).astype(BF16)

    def sources(into):
        @pl.loop(0, 4)
        def _(t):
            here = pl.ds(pl.multiple_of(t * 256, 256), 256)
            hot = onehot[:, here]
            total = dot(amount_hi[...], hot) + dot(amount_lo[...], hot)
            for m in range(2):
                into[m, pl.ds(8, ROWS), here] = total[m * ROWS : (m + 1) * ROWS]

    first = iota((8, SEG), 0)
    own = jnp.where(first == 0, share[0], share[1])
    amounts(fades(own, (8, SEG)))

    pl.semaphore_wait(barrier, N_MEM - 1 + 15)

    def halo_copies(ref, top, bottom, slot):
        return (
            pltpu.make_async_remote_copy(
                top, ref.at[:, pl.ds(ROWS + 8, 8)], up_sem.at[0, slot], up_sem.at[1, slot],
                device_id=above, device_id_type=MESH,
            ),
            pltpu.make_async_remote_copy(
                bottom, ref.at[:, pl.ds(0, 8)], down_sem.at[0, slot], down_sem.at[1, slot],
                device_id=below, device_id_type=MESH,
            ),
        )

    edges = halo_copies(field, prior.at[:, pl.ds(0, 8)], prior.at[:, pl.ds(ROWS - 8, 8)], 0)
    for copy in edges:
        copy.start()

    sources(halo_s)
    source_edges = halo_copies(halo_s, halo_s.at[:, pl.ds(8, 8)], halo_s.at[:, pl.ds(ROWS, 8)], 1)
    for copy in source_edges:
        copy.start()

    def inside(b, v):
        row = sub * ROWS + b * BLOCK - 8 + iota(v.shape, 0)
        return jnp.where((row >= 0) & (row < N_SUB * ROWS), v, 0.0)

    load.wait()
    for copy in edges:
        copy.wait()

    @pl.loop(0, ROWS // BLOCK)
    def _(b):
        start = pl.multiple_of(b * BLOCK, BLOCK)
        for m in range(2):
            v = inside(b, field[m, pl.ds(start, BLOCK + 16), :])
            v = spread(inside(b, spread(v)))
            flown[m, pl.ds(start, BLOCK), :] = v[8 : BLOCK + 8]

    def block_of(ref, d):
        return ref.at[
            :, pl.ds(pl.multiple_of((d // 2) * 8, 8), 8),
            pl.ds(pl.multiple_of(lax.rem(d, 2) * 512, 512), 512),
        ]

    keep = pltpu.make_async_copy(block_of(flown, me), got.at[:, me], big_recv)
    keep.start()

    def send_big(low, high):
        @pl.loop(low, high)
        def _(k):
            d = plane_peer(lax.rem(k * STEP, N_MEM))
            pltpu.make_async_remote_copy(
                block_of(flown, d), got.at[:, me], big_send, big_recv,
                device_id=(d, sub), device_id_type=MESH,
            ).start()

    send_big(1, BATCHES[0])

    for copy in source_edges:
        copy.wait()

    sides = iota((8, PIX), 0)

    @pl.loop(0, ROWS // BLOCK)
    def _(b):
        start = pl.multiple_of(b * BLOCK, BLOCK)
        forecast = []
        for m in range(2):
            s = inside(b, halo_s[m, pl.ds(start, BLOCK + 16), :])
            s = s + spread(s)
            forecast.append(flown[m, pl.ds(start, BLOCK), :] + s[8 : BLOCK + 8])
        for t in range(BLOCK // 8):
            j = b * (BLOCK // 4) + 2 * t
            cell = jnp.where(sides < 4, pixel[pl.ds(j, 1), :], pixel[pl.ds(j + 1, 1), :])
            lane, part, row = cell & 127, (cell >> 7) & 7, cell >> 10
            for m in range(2):
                tile = forecast[m][8 * t : 8 * t + 8]
                found = jnp.zeros((8, PIX), F32)
                for w in range(8):
                    picked = jnp.take_along_axis(tile[:, w * 128 : (w + 1) * 128], lane, axis=1)
                    found = jnp.where(part == w, picked, found)
                found = jnp.where((sides & 3) == row, found, 0.0)
                pix[j, m : m + 1, :] = jnp.sum(found[0:4], axis=0, keepdims=True)
                pix[j + 1, m : m + 1, :] = jnp.sum(found[4:8], axis=0, keepdims=True)

    @pl.loop(1, N_MEM)
    def _(i):
        d = plane_peer(i)
        pltpu.make_async_remote_copy(
            pix.at[d], pix_in.at[me], pix_send, pix_recv, device_id=(d, sub), device_id_type=MESH
        ).start()

    send_big(BATCHES[0], BATCHES[1])
    pix_in[me] = pix[me]

    def settle(view, sem):
        pltpu.make_async_copy(view, view, sem).wait()

    settle(pix_in.at[pl.ds(0, N_MEM - 1)], pix_recv)

    seen = jnp.concatenate([pix_in[:, 0, :], pix_in[:, 1, :]], axis=0)
    average = jnp.sum(seen, axis=0, keepdims=True) / (2 * N_MEM)
    seen = seen - average
    misfit = jnp.where(iota((PIX, PIX), 0) == 0, kelvin[...] - average, 0.0)
    both = jnp.concatenate([seen, misfit], axis=0)
    gram = lax.dot_general(
        seen * weight[...], both, (((1,), (1,)), ((), ())),
        preferred_element_type=F32, precision=HIGHEST,
    )
    row, col = iota((2 * N_MEM, 256), 0), iota((2 * N_MEM, 256), 1)
    carried = jnp.where(row == me, share[0], jnp.where(row == N_MEM + me, share[1], 0.0))
    gram = jnp.where((col == 129) & (sub == 0), carried, gram)
    gram_out[...] = gram.reshape(16, 8, 256)

    def to_peers(count_from, source, target, send, recv, peer):
        @pl.loop(1, 16)
        def _(i):
            p = lax.rem(count_from + i, 16)
            pltpu.make_async_remote_copy(
                source(p), target, send, recv, device_id=peer(p), device_id_type=MESH
            ).start()

    to_peers(q, lambda p: gram_out.at[p], gram_in.at[q], gram_send, gram_recv, xy_peer)
    send_big(BATCHES[1], BATCHES[2])
    gram_in[q] = gram_out[q]
    settle(gram_in.at[pl.ds(0, 15)], gram_recv)
    part_in[zc] = jnp.sum(gram_in[...], axis=0)
    to_peers(zc, lambda p: part_in.at[zc], part_in.at[zc], part_send, part_recv, zc_peer)
    send_big(BATCHES[2], BATCHES[3])
    settle(part_in.at[pl.ds(0, 15)], part_recv)
    full[q] = jnp.sum(part_in[...], axis=0)
    to_peers(q, lambda p: full.at[q], full.at[q], full_send, full_recv, xy_peer)
    send_big(BATCHES[3], BATCHES[4])
    settle(full.at[pl.ds(0, 15)], full_recv)
    send_big(BATCHES[4], BATCHES[5])

    n = 2 * N_MEM
    total = full[...].reshape(n, 256)
    eye = jnp.where(iota((n, n), 0) == iota((n, n), 1), 1.0, 0.0)
    system = (n - 1.0) * eye + total[:, :n]
    norm = jnp.sqrt(jnp.sum(system * system, axis=(0, 1), keepdims=True))

    def parts(x):
        a = x.astype(BF16)
        x = x - a.astype(F32)
        b = x.astype(BF16)
        return a, b, (x - b.astype(F32)).astype(BF16)

    def dot6(x, y):
        (a, b, c), (d, e, f) = x, y
        left = jnp.concatenate([a, a], axis=1), jnp.concatenate([b, a], axis=1), jnp.concatenate([c, b], axis=1)
        right = jnp.concatenate([d, e], axis=0), jnp.concatenate([d, f], axis=0)
        return dot(left[0], right[0]) + (dot(left[1], right[1]) + dot(left[2], right[0]))

    def newton(_, pair):
        u, v = parts(pair[0]), parts(pair[1])
        s = parts(1.5 * eye - 0.5 * dot6(v, u))
        return dot6(u, s), dot6(s, v)

    _, v = lax.fori_loop(0, ITERS, newton, (system / norm, eye))
    root = v / jnp.sqrt(norm)
    shift = dot(root, dot(root, total[:, n:], HIGHEST), HIGHEST)[:, :1]
    transform = math.sqrt(n - 1.0) * root + shift

    fade = fades(total[:, n + 1 : n + 2], (n, SEG))
    fade_mean = jnp.sum(fade, axis=0, keepdims=True) / n
    fade = fade - fade_mean
    mixed = []
    for m in range(2):
        column = jnp.where(iota((n, n), 1) == m * N_MEM + me, transform, 0.0)
        column = jnp.sum(column, axis=1, keepdims=True)
        mixed.append(fade_mean + jnp.sum(column * fade, axis=0, keepdims=True))

    grow = jnp.where(iota((n, 8 * n), 0) == iota((n, 8 * n), 1) // 8, 1.0, 0.0).astype(BF16)
    turned_hi, turned_lo = split(jnp.transpose(transform))
    grid_lo[...] = grow
    grid_hi[...] = dot(turned_hi, grid_lo[...]).astype(BF16)
    grid_lo[...] = dot(turned_lo, grid_lo[...]).astype(BF16)

    settle(got, big_recv)
    mean = jnp.sum(got[...], axis=(0, 1)) / n
    mean2 = jnp.concatenate([mean, mean], axis=0)

    @pl.loop(0, N_MEM)
    def _(i):
        m, s = i // (N_MEM // 2), lax.rem(i, N_MEM // 2)
        pert = got[m, pl.ds(2 * s, 2)].reshape(16, 512) - mean2
        hi, lo = split(pert)
        here = pl.ds(pl.multiple_of(i * 16, 16), 16)
        got_hi[here, :] = hi
        got_lo[here, :] = lo

    same_row = lax.rem(iota((n, 8 * n), 0), 8) == lax.rem(iota((n, 8 * n), 1), 8)

    @pl.loop(0, 8)
    def _(c):
        c = lax.rem(me // 8 + c, 8)
        r, k = iota((n, n), 0), iota((n, n), 1)
        pick = (r // N_MEM) * N_MEM + 8 * c + lax.rem(r, N_MEM) // 8 == k
        pick = jnp.where(pick, 1.0, 0.0).astype(BF16)
        hi = jnp.where(same_row, dot(pick, grid_hi[...]), 0.0).astype(BF16)
        lo = jnp.where(same_row, dot(pick, grid_lo[...]), 0.0).astype(BF16)
        new = dot(hi, got_hi[...]) + (dot(hi, got_lo[...]) + dot(lo, got_hi[...]))
        new = new.reshape(2, 8, 8, 512) + mean
        back[:, pl.ds(8 * c, 8)] = new

        @pl.loop(0, 8)
        def _(i):
            d = 8 * c + lax.rem(me + i, 8)

            @pl.when(d == me)
            def _():
                pltpu.make_async_copy(back.at[:, d], block_of(out, me), back_recv).start()

            @pl.when(d != me)
            def _():
                pltpu.make_async_remote_copy(
                    back.at[:, d], block_of(out, me), back_send, back_recv,
                    device_id=(d, sub), device_id_type=MESH,
                ).start()

    amounts(jnp.where(first == 0, mixed[0], jnp.where(first == 1, mixed[1], 0.0)))
    sources(halo_t)
    mixed_edges = halo_copies(halo_t, halo_t.at[:, pl.ds(8, 8)], halo_t.at[:, pl.ds(ROWS, 8)], 2)
    for copy in mixed_edges:
        copy.start()
    for copy in mixed_edges:
        copy.wait()

    @pl.loop(0, ROWS // BLOCK)
    def _(b):
        start = pl.multiple_of(b * BLOCK, BLOCK)
        for m in range(2):
            s = inside(b, halo_t[m, pl.ds(start, BLOCK + 16), :])
            s = s + spread(s)
            extra[m, pl.ds(start, BLOCK), :] = s[8 : BLOCK + 8]

    settle(got.at[:, pl.ds(0, N_MEM - 1)], big_send)
    settle(pix.at[pl.ds(0, N_MEM - 1)], pix_send)
    settle(gram_out.at[pl.ds(0, 15)], gram_send)
    settle(part_in.at[pl.ds(0, 15)], part_send)
    settle(full.at[pl.ds(0, 15)], full_send)
    settle(back.at[:, pl.ds(0, N_MEM - 1)], back_send)
    settle(out, back_recv)


def body(prior, share, cells, steps, pixel, kelvin, weight):
    vmem, any_space = pl.BlockSpec(memory_space=pltpu.VMEM), pl.BlockSpec(memory_space=pl.ANY)
    dma = pltpu.SemaphoreType.DMA
    shape = jax.ShapeDtypeStruct((2, ROWS, COLS), F32)
    n = 2 * N_MEM
    returned, extra = pl.pallas_call(
        kernel,
        out_shape=(shape, shape),
        in_specs=[any_space, pl.BlockSpec(memory_space=pltpu.SMEM)] + [vmem] * 5,
        out_specs=(any_space, vmem),
        scratch_shapes=[
            pltpu.VMEM((2, ROWS + 16, COLS), F32),
            pltpu.VMEM((2, ROWS + 16, COLS), F32),
            pltpu.VMEM((2, ROWS + 16, COLS), F32),
            pltpu.VMEM((2, ROWS, COLS), F32),
            pltpu.VMEM((SEG * RAYS, COLS), BF16),
            pltpu.VMEM((2 * ROWS, SEG * RAYS), BF16),
            pltpu.VMEM((2 * ROWS, SEG * RAYS), BF16),
            pltpu.VMEM((N_MEM, 2, PIX), F32),
            pltpu.VMEM((N_MEM, 2, PIX), F32),
            pltpu.VMEM((16, 8, 256), F32),
            pltpu.VMEM((16, 8, 256), F32),
            pltpu.VMEM((16, 8, 256), F32),
            pltpu.VMEM((16, 8, 256), F32),
            pltpu.VMEM((2, N_MEM, 8, 512), F32),
            pltpu.VMEM((8 * n, 512), BF16),
            pltpu.VMEM((8 * n, 512), BF16),
            pltpu.VMEM((n, 8 * n), BF16),
            pltpu.VMEM((n, 8 * n), BF16),
            pltpu.VMEM((2, N_MEM, 8, 512), F32),
            dma,
            dma((2, 3)),
            dma((2, 3)),
        ]
        + [dma] * 12,
        compiler_params=pltpu.CompilerParams(
            collective_id=0, has_side_effects=True, vmem_limit_bytes=56 * 2**20
        ),
    )(prior, share, cells[0].T, steps, pixel[0], kelvin[0], weight[0])
    return returned + extra


def solution(mesh):
    placed = (
        P("mem", "sub", None),
        P("mem"),
        P("sub", None, None),
        P("sub", None),
        P("sub", None, None),
        P("sub", "mem", None),
        P("sub", "mem", None),
    )
    return jax.shard_map(
        body, mesh=mesh, in_specs=placed, out_specs=P("mem", "sub", None), check_vma=False
    )
```

time: 602 us -> 131 us (0.22)
  waiting for transfers between devices: 209 us -> 0 us
  blocking collectives: 134 us -> 0 us
  Pallas kernels: 0 us -> 127 us
  local copies, waits for them, and re-layouts: 95.8 us -> 0 us
  other arithmetic: 99.7 us -> 4.1 us
  starting transfers between devices: 25.4 us -> 0 us
  matrix products: 20.1 us -> 0 us
  between operations: 14.4 us -> 0.01 us
    psum x1 -> x0, waiting for transfers between devices: 158 us -> none  [body(): gram_sum, pull_sum = lax.psum((gram_part, pull_part), ('mem', 'sub'))]
    pallas_call x0 -> x1, Pallas kernels: none -> 127 us  [body(): pl.pallas_call(kernel, out_shape=(shape, shape), in_specs=[any_space, pl....]
    scatter-add x3 -> x0, other arithmetic: 84 us -> none  [body(): melting_power_feed = jnp.zeros((realization_parts, tile_stripes * upward_...]
    psum x1 -> x0, blocking collectives: 77.3 us -> none  [body(): gram_sum, pull_sum = lax.psum((gram_part, pull_part), ('mem', 'sub'))]
    reshape x2 -> x0, local copies, waits for them, and re-layouts: 74.3 us -> none  [the longest x1 72.7 us: body(): melting_power_feed.reshape(realization_parts, tile_stripes, upward_reach)]
    all_to_all x1 -> x0, blocking collectives: 57 us -> none  [body(): lax.all_to_all(analysed, 'mem', split_axis=0, concat_axis=1, tiled=True)]
    all_to_all x1 -> x0, waiting for transfers between devices: 50.5 us -> none  [body(): lax.all_to_all(flat_field, 'mem', split_axis=1, concat_axis=0, tiled=True)]
    dot_general x65 -> x0, matrix products: 20.1 us -> none  [the longest x20 5.67 us: newton_body(): jnp.dot(upper_iter, newton_step, precision=lax.Precision.HIGHEST)]
  transfers between devices with their start and end apart: 6 -> 0, of which waited for: 3 -> 0; matrix products, arithmetic and copies ran while one was open for 27% -> 0% of each run, Pallas kernels for 0% -> 0%
where the time goes in v1:
time: 131 us
  Pallas kernels  127 us (97%)
  other arithmetic  4.1 us (3%)
    pallas_call x1, Pallas kernels, body(): pl.pallas_call(kernel, out_shape=(shape, shape), in_specs=[any_space, pl....  127 us
    add x1, other arithmetic, body(): return returned + extra  4.1 us

profile of v1, /device:TPU:1, one launch (start us, length us, event | category | flops | bytes accessed | tf_op | source)
XLA Modules:
  0.0 131.0 jit_solution(10646354165901076227)
XLA Ops:
  0.0 126.9 %shard_map.73 = (f32[2,256,1024]{2,1,0:T(8,128)}, f32[2,256,1024]{2,1,0:T(8,128)}) custom-call(f32[2,256,1024]{2,1,0:T(8,128)} %prior.1, f32[2]{0:T(128)} %share.1, s32[32,64]{1,0:T(8,128)} %bitcast.7, s32[1,64]{1,0:T(1,128)} %steps.1, s32[64,128]{1,0:T(8,128)} %bitcast.6, f32[1,128]{1,0:T(1,128)} %bitcast.8, f32[1,128]{1,0:T(1,128)} %bitcast.9), custom_call_target="tpu_custom_call" | custom-call | tf_op jit(solution)/shard_map/pallas_call | solution.py:385
  126.9 4.1 %add.3 = f32[2,256,1024]{2,1,0:T(8,128)} add(f32[2,256,1024]{2,1,0:T(8,128)} %get-tuple-element.7, f32[2,256,1024]{2,1,0:T(8,128)} %get-tuple-element.8) | non-fusion elementwise | flops 524288 | bytes 6291456 | tf_op jit(solution)/shard_map/add | solution.py:419

commit v2 on v1

--- a/solution.py
+++ b/solution.py
@@ -18,8 +18,9 @@
 SEG, RAYS = 32, 64
 PIX = 128
 BLOCK = 32
+INNER = 24
 STEP = 27
-BATCHES = (12, 19, 26, 33, 40, 64)
+BATCHES = (24, 36, 38, 48, 56, 64)
 
 
 def dot(a, b, precision=None):
@@ -54,12 +55,12 @@
 
 
 def kernel(
-    prior, share, cells, steps, pixel, kelvin, weight,
-    out, extra,
-    field, halo_s, halo_t, flown, onehot, amount_hi, amount_lo,
+    prior, share, cells_in, steps_in, pixel_in, kelvin_in, weight_in,
+    out,
+    extra, cells, steps, pixel, kelvin, weight, field, halo_s, halo_t, flown, onehot, amount,
     pix, pix_in, gram_out, gram_in, part_in, full,
     got, got_hi, got_lo, grid_hi, grid_lo, back,
-    load_sem, up_sem, down_sem, big_send, big_recv, pix_send, pix_recv,
+    load_sem, small_sem, up_sem, down_sem, big_send, big_recv, pix_send, pix_recv,
     gram_send, gram_recv, part_send, part_recv, full_send, full_recv, back_send, back_recv,
 ):
     me, sub = lax.axis_index("mem"), lax.axis_index("sub")
@@ -90,45 +91,14 @@
 
     load = pltpu.make_async_copy(prior, field.at[:, pl.ds(8, ROWS)], load_sem)
     load.start()
-
-    lanes = iota((RAYS, COLS), 1)
-    upright = jnp.transpose(cells[...])
-    for k in range(SEG):
-        col = upright[:, k : k + 1] & (COLS - 1)
-        onehot[k * RAYS : (k + 1) * RAYS, :] = jnp.where(lanes == col, 1.0, 0.0).astype(BF16)
-
-    quad = [
-        jnp.concatenate([cells[4 * c + i : 4 * c + i + 1, :] for i in range(4)], axis=1)
-        for c in range(8)
+    small = [
+        pltpu.make_async_copy(source, target, small_sem.at[i])
+        for i, (source, target) in enumerate((
+            (cells_in, cells), (steps_in, steps), (pixel_in, pixel), (kelvin_in, kelvin), (weight_in, weight)
+        ))
     ]
-    live_steps = jnp.concatenate([steps[...]] * 4, axis=1)
-
-    def amounts(fade8):
-        for c in range(8):
-            step = iota((SEG, 256), 1) // RAYS + 4 * c
-            grown = jnp.where(iota((SEG, 256), 0) == step, 1.0, 0.0)
-            value = dot(fade8, grown, HIGHEST)
-            value = jnp.where(step[:1] < live_steps, value, 0.0)
-            hit = iota((ROWS, 256), 0) == (quad[c] >> 10)
-            for m in range(2):
-                row = value[m : m + 1, :]
-                hi = row.astype(BF16).astype(F32)
-                here = (slice(m * ROWS, (m + 1) * ROWS), slice(c * 256, (c + 1) * 256))
-                amount_hi[here] = jnp.where(hit, hi, 0.0).astype(BF16)
-                amount_lo[here] = jnp.where(hit, row - hi, 0.0).astype(BF16)
-
-    def sources(into):
-        @pl.loop(0, 4)
-        def _(t):
-            here = pl.ds(pl.multiple_of(t * 256, 256), 256)
-            hot = onehot[:, here]
-            total = dot(amount_hi[...], hot) + dot(amount_lo[...], hot)
-            for m in range(2):
-                into[m, pl.ds(8, ROWS), here] = total[m * ROWS : (m + 1) * ROWS]
-
-    first = iota((8, SEG), 0)
-    own = jnp.where(first == 0, share[0], share[1])
-    amounts(fades(own, (8, SEG)))
+    for copy in small:
+        copy.start()
 
     pl.semaphore_wait(barrier, N_MEM - 1 + 15)
 
@@ -148,35 +118,24 @@
     for copy in edges:
         copy.start()
 
-    sources(halo_s)
-    source_edges = halo_copies(halo_s, halo_s.at[:, pl.ds(8, 8)], halo_s.at[:, pl.ds(ROWS, 8)], 1)
-    for copy in source_edges:
-        copy.start()
-
     def inside(b, v):
         row = sub * ROWS + b * BLOCK - 8 + iota(v.shape, 0)
         return jnp.where((row >= 0) & (row < N_SUB * ROWS), v, 0.0)
 
     load.wait()
-    for copy in edges:
-        copy.wait()
-
-    @pl.loop(0, ROWS // BLOCK)
+
+    @pl.loop(0, (ROWS - 16) // INNER)
     def _(b):
-        start = pl.multiple_of(b * BLOCK, BLOCK)
+        start = pl.multiple_of(8 + b * INNER, 8)
         for m in range(2):
-            v = inside(b, field[m, pl.ds(start, BLOCK + 16), :])
-            v = spread(inside(b, spread(v)))
-            flown[m, pl.ds(start, BLOCK), :] = v[8 : BLOCK + 8]
+            v = spread(spread(field[m, pl.ds(start, INNER + 16), :]))
+            flown[m, pl.ds(start, INNER), :] = v[8 : INNER + 8]
 
     def block_of(ref, d):
         return ref.at[
             :, pl.ds(pl.multiple_of((d // 2) * 8, 8), 8),
             pl.ds(pl.multiple_of(lax.rem(d, 2) * 512, 512), 512),
         ]
-
-    keep = pltpu.make_async_copy(block_of(flown, me), got.at[:, me], big_recv)
-    keep.start()
 
     def send_big(low, high):
         @pl.loop(low, high)
@@ -187,7 +146,68 @@
                 device_id=(d, sub), device_id_type=MESH,
             ).start()
 
+    for copy in edges:
+        copy.wait()
+    for start in (0, ROWS - 8):
+        row = sub * ROWS + start - 8 + iota((24, COLS), 0)
+        real = (row >= 0) & (row < N_SUB * ROWS)
+        for m in range(2):
+            v = jnp.where(real, field[m, start : start + 24, :], 0.0)
+            v = spread(jnp.where(real, spread(v), 0.0))
+            flown[m, start : start + 8, :] = v[8:16]
+
+    keep = pltpu.make_async_copy(block_of(flown, me), got.at[:, me], big_recv)
+    keep.start()
     send_big(1, BATCHES[0])
+
+    for copy in small:
+        copy.wait()
+
+    lanes = iota((RAYS, COLS), 1)
+    upright = jnp.transpose(cells[...])
+    for k in range(SEG):
+        col = upright[:, k : k + 1] & (COLS - 1)
+        onehot[k * RAYS : (k + 1) * RAYS, :] = jnp.where(lanes == col, 1.0, 0.0).astype(BF16)
+
+    quad = [
+        jnp.concatenate([cells[4 * c + i : 4 * c + i + 1, :] for i in range(4)], axis=1)
+        for c in range(8)
+    ]
+    live_steps = jnp.concatenate([steps[...]] * 4, axis=1)
+
+    def amounts(fade8):
+        for c in range(8):
+            step = iota((SEG, 256), 1) // RAYS + 4 * c
+            grown = jnp.where(iota((SEG, 256), 0) == step, 1.0, 0.0)
+            value = dot(fade8, grown, HIGHEST)
+            value = jnp.where(step[:1] < live_steps, value, 0.0)
+            hit = iota((ROWS, 256), 0) == (quad[c] >> 10)
+            for m in range(2):
+                row = value[m : m + 1, :]
+                hi = row.astype(BF16).astype(F32)
+                for part, piece in enumerate((hi, row - hi)):
+                    top = (2 * part + m) * ROWS
+                    amount[top : top + ROWS, c * 256 : (c + 1) * 256] = jnp.where(
+                        hit, piece, 0.0
+                    ).astype(BF16)
+
+    def sources(into):
+        @pl.loop(0, 4)
+        def _(t):
+            here = pl.ds(pl.multiple_of(t * 256, 256), 256)
+            total = dot(amount[...], onehot[:, here])
+            total = total[: 2 * ROWS] + total[2 * ROWS :]
+            for m in range(2):
+                into[m, pl.ds(8, ROWS), here] = total[m * ROWS : (m + 1) * ROWS]
+
+    first = iota((8, SEG), 0)
+    own = jnp.where(first == 0, share[0], share[1])
+    amounts(fades(own, (8, SEG)))
+
+    sources(halo_s)
+    source_edges = halo_copies(halo_s, halo_s.at[:, pl.ds(8, 8)], halo_s.at[:, pl.ds(ROWS, 8)], 1)
+    for copy in source_edges:
+        copy.start()
 
     for copy in source_edges:
         copy.wait()
@@ -376,25 +396,36 @@
     settle(back.at[:, pl.ds(0, N_MEM - 1)], back_send)
     settle(out, back_recv)
 
+    @pl.loop(0, ROWS // BLOCK)
+    def _(b):
+        here = pl.ds(pl.multiple_of(b * BLOCK, BLOCK), BLOCK)
+        for m in range(2):
+            out[m, here, :] += extra[m, here, :]
+
 
 def body(prior, share, cells, steps, pixel, kelvin, weight):
     vmem, any_space = pl.BlockSpec(memory_space=pltpu.VMEM), pl.BlockSpec(memory_space=pl.ANY)
     dma = pltpu.SemaphoreType.DMA
     shape = jax.ShapeDtypeStruct((2, ROWS, COLS), F32)
     n = 2 * N_MEM
-    returned, extra = pl.pallas_call(
+    return pl.pallas_call(
         kernel,
-        out_shape=(shape, shape),
-        in_specs=[any_space, pl.BlockSpec(memory_space=pltpu.SMEM)] + [vmem] * 5,
-        out_specs=(any_space, vmem),
+        out_shape=shape,
+        in_specs=[any_space, pl.BlockSpec(memory_space=pltpu.SMEM)] + [any_space] * 5,
+        out_specs=vmem,
         scratch_shapes=[
+            pltpu.VMEM((2, ROWS, COLS), F32),
+            pltpu.VMEM((SEG, RAYS), I32),
+            pltpu.VMEM((1, RAYS), I32),
+            pltpu.VMEM((N_MEM, PIX), I32),
+            pltpu.VMEM((1, PIX), F32),
+            pltpu.VMEM((1, PIX), F32),
             pltpu.VMEM((2, ROWS + 16, COLS), F32),
             pltpu.VMEM((2, ROWS + 16, COLS), F32),
             pltpu.VMEM((2, ROWS + 16, COLS), F32),
             pltpu.VMEM((2, ROWS, COLS), F32),
             pltpu.VMEM((SEG * RAYS, COLS), BF16),
-            pltpu.VMEM((2 * ROWS, SEG * RAYS), BF16),
-            pltpu.VMEM((2 * ROWS, SEG * RAYS), BF16),
+            pltpu.VMEM((4 * ROWS, SEG * RAYS), BF16),
             pltpu.VMEM((N_MEM, 2, PIX), F32),
             pltpu.VMEM((N_MEM, 2, PIX), F32),
             pltpu.VMEM((16, 8, 256), F32),
@@ -408,15 +439,15 @@
             pltpu.VMEM((n, 8 * n), BF16),
             pltpu.VMEM((2, N_MEM, 8, 512), F32),
             dma,
+            dma((5,)),
             dma((2, 3)),
             dma((2, 3)),
         ]
         + [dma] * 12,
         compiler_params=pltpu.CompilerParams(
-            collective_id=0, has_side_effects=True, vmem_limit_bytes=56 * 2**20
+            collective_id=0, has_side_effects=True, vmem_limit_bytes=57 * 2**20
         ),
     )(prior, share, cells[0].T, steps, pixel[0], kelvin[0], weight[0])
-    return returned + extra
 
 
 def solution(mesh):

time: 131 us -> 124 us (0.947)
  Pallas kernels: 127 us -> 121 us
  other arithmetic: 4.1 us -> 0 us
  local copies, waits for them, and re-layouts: 0 us -> 3.16 us
    pallas_call x1, Pallas kernels: 127 us -> 121 us  [body(): pl.pallas_call(kernel, out_shape=shape, in_specs=[any_space, pl.BlockSpec...]
    add x1 -> x0, other arithmetic: 4.1 us -> none  [body(): return returned + extra]
    unnamed x0 -> x1, local copies, waits for them, and re-layouts: none -> 3.16 us
where the time goes in v2:
time: 124 us
  Pallas kernels  121 us (98%)
  local copies, waits for them, and re-layouts  3.16 us (3%)
    pallas_call x1, Pallas kernels, body(): pl.pallas_call(kernel, out_shape=shape, in_specs=[any_space, pl.BlockSpec...  121 us
    unnamed x1, local copies, waits for them, and re-layouts  3.16 us

profile of v2, /device:TPU:1, one launch (start us, length us, event | category | flops | bytes accessed | tf_op | source)
XLA Modules:
  0.0 124.2 jit_solution(3221249711997332328)
XLA Ops:
  0.0 121.0 %shard_map.73 = f32[2,256,1024]{2,1,0:T(8,128)} custom-call(f32[2,256,1024]{2,1,0:T(8,128)} %prior.1, f32[2]{0:T(128)} %share.1, s32[32,64]{1,0:T(8,128)} %bitcast.7, s32[1,64]{1,0:T(1,128)} %steps_in.1, s32[64,128]{1,0:T(8,128)} %bitcast.6, f32[1,128]{1,0:T(1,128)} %bitcast.8, f32[1,128]{1,0:T(1,128)} %bitcast.9), custom_call_target="tpu_custom_call" | custom-call | tf_op jit(solution)/shard_map/pallas_call | solution.py:411
  121.0 3.2 %copy.9 = f32[2,256,1024]{2,1,0:T(8,128)} copy(f32[2,256,1024]{2,1,0:T(8,128)} %shard_map.73) | data formatting | bytes 4194304

commit v3 on v2

--- a/solution.py
+++ b/solution.py
@@ -20,6 +20,7 @@
 BLOCK = 32
 INNER = 24
 STEP = 27
+FIRST = 12
 BATCHES = (24, 36, 38, 48, 56, 64)
 
 
@@ -55,12 +56,12 @@
 
 
 def kernel(
-    prior, share, cells_in, steps_in, pixel_in, kelvin_in, weight_in,
+    prior, whole, real,
     out,
-    extra, cells, steps, pixel, kelvin, weight, field, halo_s, halo_t, flown, onehot, amount,
+    extra, field, halo_s, halo_t, flown, onehot, amount,
     pix, pix_in, gram_out, gram_in, part_in, full,
-    got, got_hi, got_lo, grid_hi, grid_lo, back,
-    load_sem, small_sem, up_sem, down_sem, big_send, big_recv, pix_send, pix_recv,
+    got, got_hi, got_lo, grid_hi, grid_lo, mix_hi, mix_lo, back,
+    load_sem, up_sem, down_sem, big_send, big_recv, pix_send, pix_recv,
     gram_send, gram_recv, part_send, part_recv, full_send, full_recv, back_send, back_recv,
 ):
     me, sub = lax.axis_index("mem"), lax.axis_index("sub")
@@ -91,15 +92,6 @@
 
     load = pltpu.make_async_copy(prior, field.at[:, pl.ds(8, ROWS)], load_sem)
     load.start()
-    small = [
-        pltpu.make_async_copy(source, target, small_sem.at[i])
-        for i, (source, target) in enumerate((
-            (cells_in, cells), (steps_in, steps), (pixel_in, pixel), (kelvin_in, kelvin), (weight_in, weight)
-        ))
-    ]
-    for copy in small:
-        copy.start()
-
     pl.semaphore_wait(barrier, N_MEM - 1 + 15)
 
     def halo_copies(ref, top, bottom, slot):
@@ -137,34 +129,57 @@
             pl.ds(pl.multiple_of(lax.rem(d, 2) * 512, 512), 512),
         ]
 
+    def send_block(d):
+        pltpu.make_async_remote_copy(
+            block_of(flown, d), got.at[:, me], big_send, big_recv,
+            device_id=(d, sub), device_id_type=MESH,
+        ).start()
+
+    def target(k):
+        return plane_peer(lax.rem(k * STEP, N_MEM))
+
     def send_big(low, high):
         @pl.loop(low, high)
         def _(k):
-            d = plane_peer(lax.rem(k * STEP, N_MEM))
-            pltpu.make_async_remote_copy(
-                block_of(flown, d), got.at[:, me], big_send, big_recv,
-                device_id=(d, sub), device_id_type=MESH,
-            ).start()
+            send_block(target(k))
+
+    @pl.loop(1, FIRST)
+    def _(k):
+        d = target(k)
+
+        @pl.when((d >= 2) & (d < N_MEM - 2))
+        def _():
+            send_block(d)
 
     for copy in edges:
         copy.wait()
     for start in (0, ROWS - 8):
         row = sub * ROWS + start - 8 + iota((24, COLS), 0)
-        real = (row >= 0) & (row < N_SUB * ROWS)
+        inner = (row >= 0) & (row < N_SUB * ROWS)
         for m in range(2):
-            v = jnp.where(real, field[m, start : start + 24, :], 0.0)
-            v = spread(jnp.where(real, spread(v), 0.0))
+            v = jnp.where(inner, field[m, start : start + 24, :], 0.0)
+            v = spread(jnp.where(inner, spread(v), 0.0))
             flown[m, start : start + 8, :] = v[8:16]
 
     keep = pltpu.make_async_copy(block_of(flown, me), got.at[:, me], big_recv)
     keep.start()
-    send_big(1, BATCHES[0])
-
-    for copy in small:
-        copy.wait()
+    @pl.loop(1, FIRST)
+    def _(k):
+        d = target(k)
+
+        @pl.when((d < 2) | (d >= N_MEM - 2))
+        def _():
+            send_block(d)
+
+    send_big(FIRST, BATCHES[0])
+
+    cells = whole[N_MEM : N_MEM + SEG, :RAYS]
+    steps = whole[N_MEM + SEG : N_MEM + SEG + 8, :][0:1, :RAYS]
+    kelvin, weight = real[0:1, :], real[1:2, :]
+    share = real[2:3, 0:1], real[2:3, 1:2]
 
     lanes = iota((RAYS, COLS), 1)
-    upright = jnp.transpose(cells[...])
+    upright = jnp.transpose(cells)
     for k in range(SEG):
         col = upright[:, k : k + 1] & (COLS - 1)
         onehot[k * RAYS : (k + 1) * RAYS, :] = jnp.where(lanes == col, 1.0, 0.0).astype(BF16)
@@ -173,7 +188,7 @@
         jnp.concatenate([cells[4 * c + i : 4 * c + i + 1, :] for i in range(4)], axis=1)
         for c in range(8)
     ]
-    live_steps = jnp.concatenate([steps[...]] * 4, axis=1)
+    live_steps = jnp.concatenate([steps] * 4, axis=1)
 
     def amounts(fade8):
         for c in range(8):
@@ -224,7 +239,7 @@
             forecast.append(flown[m, pl.ds(start, BLOCK), :] + s[8 : BLOCK + 8])
         for t in range(BLOCK // 8):
             j = b * (BLOCK // 4) + 2 * t
-            cell = jnp.where(sides < 4, pixel[pl.ds(j, 1), :], pixel[pl.ds(j + 1, 1), :])
+            cell = jnp.where(sides < 4, whole[pl.ds(j, 1), :], whole[pl.ds(j + 1, 1), :])
             lane, part, row = cell & 127, (cell >> 7) & 7, cell >> 10
             for m in range(2):
                 tile = forecast[m][8 * t : 8 * t + 8]
@@ -254,10 +269,10 @@
     seen = jnp.concatenate([pix_in[:, 0, :], pix_in[:, 1, :]], axis=0)
     average = jnp.sum(seen, axis=0, keepdims=True) / (2 * N_MEM)
     seen = seen - average
-    misfit = jnp.where(iota((PIX, PIX), 0) == 0, kelvin[...] - average, 0.0)
+    misfit = jnp.where(iota((PIX, PIX), 0) == 0, kelvin - average, 0.0)
     both = jnp.concatenate([seen, misfit], axis=0)
     gram = lax.dot_general(
-        seen * weight[...], both, (((1,), (1,)), ((), ())),
+        seen * weight, both, (((1,), (1,)), ((), ())),
         preferred_element_type=F32, precision=HIGHEST,
     )
     row, col = iota((2 * N_MEM, 256), 0), iota((2 * N_MEM, 256), 1)
@@ -330,11 +345,22 @@
     grid_hi[...] = dot(turned_hi, grid_lo[...]).astype(BF16)
     grid_lo[...] = dot(turned_lo, grid_lo[...]).astype(BF16)
 
+    same_row = lax.rem(iota((n, 8 * n), 0), 8) == lax.rem(iota((n, 8 * n), 1), 8)
+
+    def expand(turn):
+        c = lax.rem(me // 8 + turn, 8)
+        r, k = iota((n, n), 0), iota((n, n), 1)
+        pick = (r // N_MEM) * N_MEM + 8 * c + lax.rem(r, N_MEM) // 8 == k
+        pick = jnp.where(pick, 1.0, 0.0).astype(BF16)
+        mix_hi[...] = jnp.where(same_row, dot(pick, grid_hi[...]), 0.0).astype(BF16)
+        mix_lo[...] = jnp.where(same_row, dot(pick, grid_lo[...]), 0.0).astype(BF16)
+
+    expand(0)
     settle(got, big_recv)
     mean = jnp.sum(got[...], axis=(0, 1)) / n
     mean2 = jnp.concatenate([mean, mean], axis=0)
 
-    @pl.loop(0, N_MEM)
+    @pl.loop(0, N_MEM, unroll=4)
     def _(i):
         m, s = i // (N_MEM // 2), lax.rem(i, N_MEM // 2)
         pert = got[m, pl.ds(2 * s, 2)].reshape(16, 512) - mean2
@@ -343,16 +369,10 @@
         got_hi[here, :] = hi
         got_lo[here, :] = lo
 
-    same_row = lax.rem(iota((n, 8 * n), 0), 8) == lax.rem(iota((n, 8 * n), 1), 8)
-
     @pl.loop(0, 8)
-    def _(c):
-        c = lax.rem(me // 8 + c, 8)
-        r, k = iota((n, n), 0), iota((n, n), 1)
-        pick = (r // N_MEM) * N_MEM + 8 * c + lax.rem(r, N_MEM) // 8 == k
-        pick = jnp.where(pick, 1.0, 0.0).astype(BF16)
-        hi = jnp.where(same_row, dot(pick, grid_hi[...]), 0.0).astype(BF16)
-        lo = jnp.where(same_row, dot(pick, grid_lo[...]), 0.0).astype(BF16)
+    def _(turn):
+        c = lax.rem(me // 8 + turn, 8)
+        hi, lo = mix_hi[...], mix_lo[...]
         new = dot(hi, got_hi[...]) + (dot(hi, got_lo[...]) + dot(lo, got_hi[...]))
         new = new.reshape(2, 8, 8, 512) + mean
         back[:, pl.ds(8 * c, 8)] = new
@@ -371,6 +391,8 @@
                     back.at[:, d], block_of(out, me), back_send, back_recv,
                     device_id=(d, sub), device_id_type=MESH,
                 ).start()
+
+        expand(turn + 1)
 
     amounts(jnp.where(first == 0, mixed[0], jnp.where(first == 1, mixed[1], 0.0)))
     sources(halo_t)
@@ -408,18 +430,24 @@
     dma = pltpu.SemaphoreType.DMA
     shape = jax.ShapeDtypeStruct((2, ROWS, COLS), F32)
     n = 2 * N_MEM
+
+    def stack(pieces, rows):
+        total, top = 0, 0
+        for x in pieces:
+            below = rows - top - x.shape[0]
+            total += jnp.pad(x, ((top, below), (0, PIX - x.shape[1])))
+            top += x.shape[0]
+        return total
+
+    whole = stack((pixel[0], cells[0].T, steps), N_MEM + SEG + 8)
+    real = stack((kelvin[0], weight[0], share[None]), 8)
     return pl.pallas_call(
         kernel,
         out_shape=shape,
-        in_specs=[any_space, pl.BlockSpec(memory_space=pltpu.SMEM)] + [any_space] * 5,
+        in_specs=[any_space, vmem, vmem],
         out_specs=vmem,
         scratch_shapes=[
             pltpu.VMEM((2, ROWS, COLS), F32),
-            pltpu.VMEM((SEG, RAYS), I32),
-            pltpu.VMEM((1, RAYS), I32),
-            pltpu.VMEM((N_MEM, PIX), I32),
-            pltpu.VMEM((1, PIX), F32),
-            pltpu.VMEM((1, PIX), F32),
             pltpu.VMEM((2, ROWS + 16, COLS), F32),
             pltpu.VMEM((2, ROWS + 16, COLS), F32),
             pltpu.VMEM((2, ROWS + 16, COLS), F32),
@@ -437,17 +465,18 @@
             pltpu.VMEM((8 * n, 512), BF16),
             pltpu.VMEM((n, 8 * n), BF16),
             pltpu.VMEM((n, 8 * n), BF16),
+            pltpu.VMEM((n, 8 * n), BF16),
+            pltpu.VMEM((n, 8 * n), BF16),
             pltpu.VMEM((2, N_MEM, 8, 512), F32),
             dma,
-            dma((5,)),
             dma((2, 3)),
             dma((2, 3)),
         ]
         + [dma] * 12,
         compiler_params=pltpu.CompilerParams(
-            collective_id=0, has_side_effects=True, vmem_limit_bytes=57 * 2**20
+            collective_id=0, has_side_effects=True, vmem_limit_bytes=50 * 2**20
         ),
-    )(prior, share, cells[0].T, steps, pixel[0], kelvin[0], weight[0])
+    )(prior, whole, real)
 
 
 def solution(mesh):

time: 124 us -> 122 us (0.984)
  Pallas kernels: 121 us -> 119 us
  local copies, waits for them, and re-layouts: 3.16 us -> 1.32 us
  other arithmetic: 0 us -> 1.49 us
    unnamed x1, local copies, waits for them, and re-layouts: 3.16 us -> 1.32 us
    pallas_call x1, Pallas kernels: 121 us -> 119 us  [body(): pl.pallas_call(kernel, out_shape=shape, in_specs=[any_space, vmem, vmem],...]
    add x0 -> x2, other arithmetic: none -> 1.49 us  [stack(): total += jnp.pad(x, ((top, below), (0, PIX - x.shape[1])))]
where the time goes in v3:
time: 122 us
  Pallas kernels  119 us (98%)
  other arithmetic  1.49 us (1%)
  local copies, waits for them, and re-layouts  1.32 us (1%)
    pallas_call x1, Pallas kernels, body(): pl.pallas_call(kernel, out_shape=shape, in_specs=[any_space, vmem, vmem],...  119 us

profile of v3, /device:TPU:1, one launch (start us, length us, event | category | flops | bytes accessed | tf_op | source)
XLA Modules:
  0.0 122.1 jit_solution(9997888041854741479)
XLA Ops:
  0.0 0.7 pad_add_fusion.1.real
  0.7 0.8 pad_add_fusion.whole
  1.5 119.2 %shard_map.73 = f32[2,256,1024]{2,1,0:T(8,128)S(1)} custom-call(f32[2,256,1024]{2,1,0:T(8,128)} %prior.1, s32[104,128]{1,0:T(8,128)S(1)} %pad_add_fusion.whole, f32[8,128]{1,0:T(8,128)S(1)} %pad_add_fusion.1.real), custom_call_target="tpu_custom_call" | custom-call | tf_op jit(solution)/shard_map/pallas_call | solution.py:444
  120.7 1.3 %copy.9 = f32[2,256,1024]{2,1,0:T(8,128)} copy(f32[2,256,1024]{2,1,0:T(8,128)S(1)} %shard_map.73) | data formatting | bytes 4194304

commit v4 on v3

--- a/solution.py
+++ b/solution.py
@@ -348,7 +348,7 @@
     same_row = lax.rem(iota((n, 8 * n), 0), 8) == lax.rem(iota((n, 8 * n), 1), 8)
 
     def expand(turn):
-        c = lax.rem(me // 8 + turn, 8)
+        c = lax.rem(me // 8 + turn + 1, 8)
         r, k = iota((n, n), 0), iota((n, n), 1)
         pick = (r // N_MEM) * N_MEM + 8 * c + lax.rem(r, N_MEM) // 8 == k
         pick = jnp.where(pick, 1.0, 0.0).astype(BF16)
@@ -371,7 +371,7 @@
 
     @pl.loop(0, 8)
     def _(turn):
-        c = lax.rem(me // 8 + turn, 8)
+        c = lax.rem(me // 8 + turn + 1, 8)
         hi, lo = mix_hi[...], mix_lo[...]
         new = dot(hi, got_hi[...]) + (dot(hi, got_lo[...]) + dot(lo, got_hi[...]))
         new = new.reshape(2, 8, 8, 512) + mean

time: 122 us -> 121 us (level)
    pallas_call x1, Pallas kernels: 119 us -> 118 us  [body(): pl.pallas_call(kernel, out_shape=shape, in_specs=[any_space, vmem, vmem],...]
where the time goes in v4:
time: 121 us
  Pallas kernels  118 us (98%)
  other arithmetic  1.49 us (1%)
  local copies, waits for them, and re-layouts  1.32 us (1%)
    pallas_call x1, Pallas kernels, body(): pl.pallas_call(kernel, out_shape=shape, in_specs=[any_space, vmem, vmem],...  118 us

profile of v4, /device:TPU:1, one launch (start us, length us, event | category | flops | bytes accessed | tf_op | source)
XLA Modules:
  0.0 120.7 jit_solution(200421649011818220)
XLA Ops:
  0.0 0.7 pad_add_fusion.1.real
  0.7 0.8 pad_add_fusion.whole
  1.5 117.9 %shard_map.73 = f32[2,256,1024]{2,1,0:T(8,128)S(1)} custom-call(f32[2,256,1024]{2,1,0:T(8,128)} %prior.1, s32[104,128]{1,0:T(8,128)S(1)} %pad_add_fusion.whole, f32[8,128]{1,0:T(8,128)S(1)} %pad_add_fusion.1.real), custom_call_target="tpu_custom_call" | custom-call | tf_op jit(solution)/shard_map/pallas_call | solution.py:444
  119.4 1.3 %copy.9 = f32[2,256,1024]{2,1,0:T(8,128)} copy(f32[2,256,1024]{2,1,0:T(8,128)S(1)} %shard_map.73) | data formatting | bytes 4194304
